TPU v7x, 32 devices: a whole 2x2x4 slice. The times are simulated.
32 devices in a mesh: dst: 16 (over z, x, core), tok: 2 (over y).
Axes of the slice: x: 2, y: 2, z: 4, core: 2. Of those that a mesh axis runs over, the one named last changes fastest.
Arguments:
- latents: float32 [2048, 32768], P('tok', 'dst'), may hold values from 0 to 0.2, as said below
- mask: int32 [2048, 32768], P('tok', 'dst'), may hold values from 0 to 1
- errors: bfloat16 [2048, 4, 2048], P('tok'), may hold values from -6 to 6
- decoder: bfloat16 [32768, 4, 2048], P('dst'), may hold values from -0.125 to 0.125
Outputs:
- decoder_grad: bfloat16 [32768, 4, 2048], P('dst', None, 'tok')
- latent_grad: float32 [2048, 32768], P('tok', 'dst')
Inputs may be any that keep to these rules, and one draw needn't show every extreme that they name: `latents`: zero exactly where mask is 0 and positive where mask is 1.
All inputs are finite; a program needn't handle non-finite values.
Results may differ from a plain program's by a relative error of at most 0.001.
Values may be sent and summed in bfloat16 or wider, within the bound.
A program may use at most 384 MiB of HBM per device.

v0:
```python
import jax
import jax.numpy as jnp
from jax import lax
from jax.sharding import PartitionSpec as P

LAYERS = 4


def shifted(array, axis, by):
    peers = lax.axis_size(axis)
    pairs = [(i, i + by) for i in range(peers) if 0 <= i + by < peers]
    return lax.ppermute(array, axis, pairs)


def latent_terms(sources, errors_used):
    errors_wide = errors_used.astype(jnp.float32)
    blocks = [
        lax.dot_general(
            source,
            errors_wide,
            (((0,), (0,)), ((), ())),
            precision=lax.Precision.HIGHEST,
            preferred_element_type=jnp.float32,
        )
        for source in sources
    ]
    return jnp.stack(blocks, axis=1)


def per_device(latents, mask, errors, decoder):
    per_group = lax.axis_size("dst") // LAYERS
    my_group = lax.axis_index("dst") // per_group
    own_errors = lax.dynamic_index_in_dim(errors, my_group, 1, keepdims=False)
    sources = [latents]
    for distance in range(1, LAYERS):
        sources.append(shifted(latents, "dst", distance * per_group))
    partials = []
    for distance in range(LAYERS):
        valid = (distance <= my_group).astype(jnp.float32)
        weights = decoder[:, distance, :]
        product = lax.dot_general(
            own_errors, weights, (((1,), (1,)), ((), ())), preferred_element_type=jnp.float32
        )
        partials.append(valid * product)
    summed = partials[0]
    for distance in range(1, LAYERS):
        summed = summed + shifted(partials[distance], "dst", -distance * per_group)
    latent_grad = mask.astype(jnp.float32) * summed
    terms = latent_terms(sources, own_errors)
    totals = lax.psum_scatter(terms, "tok", scatter_dimension=2, tiled=True)
    return (totals.astype(jnp.bfloat16), latent_grad)


def solution(mesh):
    placed = (P("tok", "dst"), P("tok", "dst"), P("tok", None, None), P("dst", None, None))
    return jax.shard_map(
        per_device,
        mesh=mesh,
        in_specs=placed,
        out_specs=(P("dst", None, "tok"), P("tok", "dst")),
        check_vma=False,
    )
```

profile of v0, /device:TPU:0, one launch (start us, length us, event | category | flops | bytes accessed | tf_op | source)
XLA Modules:
  0.0 1591.1 jit_solution(5153118750614365485)
XLA Ops:
  7.2 10.2 collective-permute-start.2
  17.4 4.5 collective-permute-start.1
  21.9 4.5 collective-permute-start
  26.4 10.4 constant_dynamic-slice_fusion
  36.9 2.8 copy.35
  40.3 29.6 %convolution_bitcast_fusion.3 = f32[2048,1,2048]{0,2,1:T(8,128)} fusion(bf16[1024,2048]{1,0:T(8,128)(2,1)S(1)} %bitcast.51, f32[1024,2048]{1,0:T(8,128)S(1)} %copy-done.1), kind=kOutput, calls=%fused_computation.4 | convolution fusion | flops 51539607552 | bytes 29360128 | tf_op jit(solution)/shard_map/dot_general | solution.py:18
  69.9 125.5 %collective-permute-done.2 = f32[1024,2048]{1,0:T(8,128)} collective-permute-done((f32[1024,2048]{1,0:T(8,128)}, f32[1024,2048]{1,0:T(8,128)}, u32[]{:S(2)}, u32[]{:S(2)}) %collective-permute-start.2) | collective-permute-done | bytes 8388640 | tf_op jit(solution)/shard_map/ppermute | solution.py:12
  195.4 31.3 %convolution_bitcast_fusion = f32[2048,1,2048]{0,2,1:T(8,128)} fusion(bf16[1024,2048]{1,0:T(8,128)(2,1)S(1)} %bitcast.52, f32[1024,2048]{1,0:T(8,128)} %collective-permute-done.2), kind=kOutput, calls=%fused_computation.1 | convolution fusion | flops 51539607552 | bytes 29360128 | tf_op jit(solution)/shard_map/dot_general | solution.py:18
  226.7 148.5 %collective-permute-done.1 = f32[1024,2048]{1,0:T(8,128)} collective-permute-done((f32[1024,2048]{1,0:T(8,128)}, f32[1024,2048]{1,0:T(8,128)}, u32[]{:S(2)}, u32[]{:S(2)}) %collective-permute-start.1) | collective-permute-done | bytes 8388640 | tf_op jit(solution)/shard_map/ppermute | solution.py:12
  375.2 31.6 %convolution_bitcast_fusion.1 = f32[2048,1,2048]{0,2,1:T(8,128)} fusion(bf16[1024,2048]{1,0:T(8,128)(2,1)S(1)} %bitcast.53, f32[1024,2048]{1,0:T(8,128)} %collective-permute-done.1), kind=kOutput, calls=%fused_computation.2 | convolution fusion | flops 51539607552 | bytes 29360128 | tf_op jit(solution)/shard_map/dot_general | solution.py:18
  406.8 147.0 %collective-permute-done = f32[1024,2048]{1,0:T(8,128)} collective-permute-done((f32[1024,2048]{1,0:T(8,128)}, f32[1024,2048]{1,0:T(8,128)}, u32[]{:S(2)}, u32[]{:S(2)}) %collective-permute-start) | collective-permute-done | bytes 8388640 | tf_op jit(solution)/shard_map/ppermute | solution.py:12
  553.8 31.2 %convolution_bitcast_fusion.2 = f32[2048,1,2048]{0,2,1:T(8,128)} fusion(bf16[1024,2048]{1,0:T(8,128)(2,1)S(1)} %bitcast.54, f32[1024,2048]{1,0:T(8,128)} %collective-permute-done), kind=kOutput, calls=%fused_computation.3 | convolution fusion | flops 51539607552 | bytes 29360128 | tf_op jit(solution)/shard_map/dot_general | solution.py:18
  585.0 43.5 %pad_maximum_fusion = f32[2048,4,2048]{0,2,1:T(8,128)} fusion(f32[2048,1,2048]{0,2,1:T(8,128)} %convolution_bitcast_fusion, f32[2048,1,2048]{0,2,1:T(8,128)} %convolution_bitcast_fusion.1, f32[2048,1,2048]{0,2,1:T(8,128)} %convolution_bitcast_fusion.2, f32[2048,1,2048]{0,2,1:T(8,128)} %convolution_bitcast_fusion.3), kind=kLoop, calls=%fused_computation | loop fusion | flops 50331648 | bytes 134217728 | tf_op jit(solution)/shard_map/stack | solution.py:27
  628.6 79.6 %fusion.7 = (bf16[2048,1,2048]{2,1,0:T(2,128)(2,1)}, bf16[2048,1,2048]{2,1,0:T(2,128)(2,1)}, bf16[2048,1,2048]{2,1,0:T(2,128)(2,1)}, bf16[2048,1,2048]{2,1,0:T(2,128)(2,1)}) fusion(bf16[2048,4,2048]{2,1,0:T(4,128)(2,1)} %param.7), kind=kLoop, calls=%fused_computation.19 | loop fusion | bytes 67108864 | tf_op jit(solution)/shard_map/slice | solution.py:40
  708.2 16.4 %fusion.6 = f32[1024,2048]{1,0:T(8,128)} fusion(bf16[1024,2048]{1,0:T(8,128)(2,1)} %bitcast.55, bf16[2048,1,2048]{2,1,0:T(2,128)(2,1)} %get-tuple-element.9, f32[]{:T(128)S(6)} %convert_element_type.24), kind=kOutput, calls=%fused_computation.16 | convolution fusion | flops 8592031744 | bytes 20971524 | tf_op jit(solution)/shard_map/dot_general | solution.py:41
  725.9 16.1 %fusion.5 = f32[1024,2048]{1,0:T(8,128)} fusion(bf16[1024,2048]{1,0:T(8,128)(2,1)} %bitcast.56, bf16[2048,1,2048]{2,1,0:T(2,128)(2,1)} %get-tuple-element.7, f32[]{:T(128)S(6)} %convert_element_type.23), kind=kOutput, calls=%fused_computation.15 | convolution fusion | flops 8592031744 | bytes 20971524 | tf_op jit(solution)/shard_map/dot_general | solution.py:41
  743.3 16.4 %fusion.4 = f32[1024,2048]{1,0:T(8,128)} fusion(bf16[1024,2048]{1,0:T(8,128)(2,1)} %bitcast.57, bf16[2048,1,2048]{2,1,0:T(2,128)(2,1)} %get-tuple-element.8, f32[]{:T(128)S(6)} %convert_element_type.22), kind=kOutput, calls=%fused_computation.14 | convolution fusion | flops 8592031744 | bytes 20971524 | tf_op jit(solution)/shard_map/dot_general | solution.py:41
  761.0 182.5 %collective-permute-done.5 = f32[1024,2048]{1,0:T(8,128)} collective-permute-done((f32[1024,2048]{1,0:T(8,128)}, f32[1024,2048]{1,0:T(8,128)}, u32[]{:S(2)}, u32[]{:S(2)}) %collective-permute-start.5) | collective-permute-done | bytes 8388640 | tf_op jit(solution)/shard_map/ppermute | solution.py:12
  943.5 358.8 %collective-permute-done.4 = f32[1024,2048]{1,0:T(8,128)} collective-permute-done((f32[1024,2048]{1,0:T(8,128)}, f32[1024,2048]{1,0:T(8,128)}, u32[]{:S(2)}, u32[]{:S(2)}) %collective-permute-start.4) | collective-permute-done | bytes 8388640 | tf_op jit(solution)/shard_map/ppermute | solution.py:12
  1302.4 4.0 collective-permute-done.3
  1306.3 25.0 %add_multiply_fusion = f32[1024,2048]{1,0:T(8,128)} fusion(f32[1024,2048]{1,0:T(8,128)} %collective-permute-done.5, f32[1024,2048]{1,0:T(8,128)} %collective-permute-done.4, f32[1024,2048]{1,0:T(8,128)} %collective-permute-done.3, s32[1024,2048]{1,0:T(8,128)} %param.5, bf16[1024,2048]{1,0:T(8,128)(2,1)} %bitcast.58, ...), kind=kOutput, calls=%fused_computation.13 | convolution fusion | flops 8602517504 | bytes 54525956 | tf_op jit(solution)/shard_map/dot_general | solution.py:41
  1331.3 206.6 %reduce-scatter.2.cloned.1.call-done = f32[2048,4,1024]{0,2,1:T(8,128)} async-done(((f32[2048,4,2048]{0,2,1:T(8,128)}), f32[2048,4,1024]{0,2,1:T(8,128)}) %reduce-scatter.2.cloned.1.call-update) | async-done | bytes 33554448 | tf_op jit(solution)/shard_map/reduce_scatter | solution.py:50
  1537.9 17.5 %convert_element_type.19 = bf16[2048,4,1024]{0,2,1:T(8,128)(2,1)} convert(f32[2048,4,1024]{0,2,1:T(8,128)} %reduce-scatter.2.cloned.1.call-done) | non-fusion elementwise | flops 8388608 | bytes 50331648 | tf_op jit(solution)/shard_map/convert_element_type | solution.py:51
  1555.4 28.5 %copy.12 = bf16[2048,4,1024]{2,1,0:T(4,128)(2,1)} copy(bf16[2048,4,1024]{0,2,1:T(8,128)(2,1)} %convert_element_type.19) | data formatting | bytes 33554432
  (9 shorter events, 4.5 us)
Async XLA Ops:
  7.2 1530.8 %reduce-scatter.2.cloned.1.call-start = ((), (), s32[]{:S(2)}) async-start(), calls=%async_computation.1 | async-start | bytes 100663296 | tf_op jit(solution)/shard_map/reduce_scatter | solution.py:50
  7.2 188.2 %collective-permute-start.2 = (f32[1024,2048]{1,0:T(8,128)}, f32[1024,2048]{1,0:T(8,128)}, u32[]{:S(2)}, u32[]{:S(2)}) collective-permute-start(f32[1024,2048]{1,0:T(8,128)} %param.4), channel_id=1, source_target_pairs={{0,24},{2,26},{4,28},{6,30},{1,25},{3,27},{5,29},{7,31}} | collective-permute-start | bytes 25165832 | tf_op jit(solution)/shard_map/ppermute | solution.py:12
  17.4 357.8 %collective-permute-start.1 = (f32[1024,2048]{1,0:T(8,128)}, f32[1024,2048]{1,0:T(8,128)}, u32[]{:S(2)}, u32[]{:S(2)}) collective-permute-start(f32[1024,2048]{1,0:T(8,128)} %param.4), channel_id=1, source_target_pairs={{0,16},{2,18},{4,20},{6,22},{8,24},{10,26},{12,28},{14,30},{1,17},... | collective-permute-start | bytes 25165832 | tf_op jit(solution)/shard_map/ppermute | solution.py:12
  21.9 531.9 %collective-permute-start = (f32[1024,2048]{1,0:T(8,128)}, f32[1024,2048]{1,0:T(8,128)}, u32[]{:S(2)}, u32[]{:S(2)}) collective-permute-start(f32[1024,2048]{1,0:T(8,128)} %param.4), channel_id=1, source_target_pairs={{0,8},{2,10},{4,12},{6,14},{8,16},{10,18},{12,20},{14,22},{16,24},... | collective-permute-start | bytes 25165832 | tf_op jit(solution)/shard_map/ppermute | solution.py:12
  36.9 3.4 copy-start.1
  39.7 514.2 %copy-start = (bf16[1024,1,2048]{2,0,1:T(8,128)(2,1)}, bf16[1024,1,2048]{2,0,1:T(8,128)(2,1)S(1)}, u32[]{:S(2)}) copy-start(bf16[1024,1,2048]{2,0,1:T(8,128)(2,1)S(1)} %copy.35) | copy-start | bytes 12582916
  724.6 218.9 %collective-permute-start.5 = (f32[1024,2048]{1,0:T(8,128)}, f32[1024,2048]{1,0:T(8,128)}, u32[]{:S(2)}, u32[]{:S(2)}) collective-permute-start(f32[1024,2048]{1,0:T(8,128)} %fusion.6), channel_id=1, source_target_pairs={{24,0},{26,2},{28,4},{30,6},{25,1},{27,3},{29,5},{31,7}} | collective-permute-start | bytes 25165832 | tf_op jit(solution)/shard_map/ppermute | solution.py:12
  742.0 560.3 %collective-permute-start.4 = (f32[1024,2048]{1,0:T(8,128)}, f32[1024,2048]{1,0:T(8,128)}, u32[]{:S(2)}, u32[]{:S(2)}) collective-permute-start(f32[1024,2048]{1,0:T(8,128)} %fusion.5), channel_id=1, source_target_pairs={{16,0},{18,2},{20,4},{22,6},{24,8},{26,10},{28,12},{30,14},{17,1},... | collective-permute-start | bytes 25165832 | tf_op jit(solution)/shard_map/ppermute | solution.py:12
  759.7 546.6 %collective-permute-start.3 = (f32[1024,2048]{1,0:T(8,128)}, f32[1024,2048]{1,0:T(8,128)}, u32[]{:S(2)}, u32[]{:S(2)}) collective-permute-start(f32[1024,2048]{1,0:T(8,128)} %fusion.4), channel_id=1, source_target_pairs={{8,0},{10,2},{12,4},{14,6},{16,8},{18,10},{20,12},{22,14},{24,16},... | collective-permute-start | bytes 25165832 | tf_op jit(solution)/shard_map/ppermute | solution.py:12
Sparse Core Ops, SparseCore 0:
  628.7 909.1 reduce-scatter.1
where the time goes:
time: 1600 us; the launch traced here: 1590 us
  waiting for transfers between devices  1170 us (73%)
  matrix products  198 us (12%)
  local copies, waits for them, and re-layouts  122 us (8%)
  other arithmetic  61 us (4%)
  starting transfers between devices  23.1 us (1%)
    ppermute x6, waiting for transfers between devices, shifted(): return lax.ppermute(array, axis, pairs)  966 us
    reduce_scatter x1, waiting for transfers between devices, per_device(): totals = lax.psum_scatter(terms, 'tok', scatter_dimension=2, tiled=True)  207 us
    dot_general x4, matrix products, latent_terms(): lax.dot_general(source, errors_wide, (((0,), (0,)), ((), ())), precision=...  124 us
    slice x1, local copies, waits for them, and re-layouts, per_device(): weights = decoder[:, distance, :]  79.6 us
    dot_general x4, matrix products, per_device(): lax.dot_general(own_errors, weights, (((1,), (1,)), ((), ())), preferred_...  73.9 us
    another operation x1, other arithmetic, latent_terms(): return jnp.stack(blocks, axis=1)  43.5 us
  transfers between devices with their start and end apart: 7, of which 7 were waited for; matrix products, arithmetic and copies ran while one was open for 16% of the time, Pallas kernels for 0%

commit v1 on v0

v1 whole, which is shorter than its diff:
```python
import jax
import jax.numpy as jnp
from jax import lax
from jax.experimental import pallas as pl
from jax.experimental.layout import Layout, with_layout_constraint
from jax.experimental.pallas import tpu as pltpu
from jax.sharding import PartitionSpec as P

LAYERS = 4
CHUNKS = 4
SUM_CHUNKS = 4
TILE = 256
LEVELS = 65535.0
HALF = 32768


def group_shift(array, by, first, last):
    per_group = lax.axis_size("dst") // LAYERS
    pairs = [
        (group * per_group + i, (group + by) * per_group + i)
        for group in range(first, last + 1)
        for i in range(per_group)
    ]
    return lax.ppermute(array, "dst", pairs)


def tok_shift(array, by):
    peers = lax.axis_size("tok")
    return lax.ppermute(array, "tok", [(i, (i + by) % peers) for i in range(peers)])


def after(array, ready):
    return lax.optimization_barrier((array, ready))[0]


def product_kernel(parts, step_ref, *refs):
    total = None
    for part in range(parts):
        code = refs[part][...].astype(jnp.int32) + HALF
        e = refs[parts + part][...]
        for piece in (code & 0xFF00, code & 0xFF):
            exact = piece.astype(jnp.float32).astype(jnp.bfloat16)
            term = jnp.dot(exact, e, preferred_element_type=jnp.float32)
            total = term if total is None else total + term
    refs[2 * parts][...] = (step_ref[...] * total).astype(jnp.bfloat16)


def product(codes, errors, step):
    features, tokens = codes[0].shape
    width = errors[0].shape[1]
    parts = len(codes)
    tile = min(TILE, features)
    return pl.pallas_call(
        lambda *refs: product_kernel(parts, *refs),
        grid=(features // tile,),
        in_specs=[pl.BlockSpec((tile, 1), lambda i: (i, 0))]
        + [pl.BlockSpec((tile, tokens), lambda i: (i, 0))] * parts
        + [pl.BlockSpec((tokens, width), lambda i: (0, 0))] * parts,
        out_specs=pl.BlockSpec((tile, width), lambda i: (i, 0)),
        out_shape=jax.ShapeDtypeStruct((features, width), jnp.bfloat16),
        compiler_params=pltpu.CompilerParams(vmem_limit_bytes=40 * 2**20),
        cost_estimate=pl.CostEstimate(
            flops=4 * parts * features * tokens * width,
            bytes_accessed=2 * (parts * (features * tokens + tokens * width) + features * width),
            transcendentals=0,
        ),
    )(step, *codes, *errors)


def per_device(latents, mask, errors, decoder):
    toks = lax.axis_size("tok")
    tok = lax.axis_index("tok")
    per_group = lax.axis_size("dst") // LAYERS
    place = lax.axis_index("dst")
    my_group = place // per_group
    member = place % per_group
    tokens, _, depth = errors.shape
    features = latents.shape[1]
    width = depth // toks
    rows = tokens // per_group
    members = [list(range(g * per_group, (g + 1) * per_group)) for g in range(LAYERS)]

    peak = jnp.max(latents, axis=0)
    for r in range(1, toks):
        peak = jnp.maximum(peak, tok_shift(peak, r))
    peak = jnp.maximum(peak, 1e-30)
    step = peak * (1.0 / LEVELS)
    per_step = LEVELS / peak

    ahead = LAYERS - 1
    layers = [
        lax.dynamic_index_in_dim(errors, jnp.minimum(my_group + j, LAYERS - 1), 1, keepdims=False)
        for j in range(ahead)
    ]

    own = [lax.dynamic_slice(e, (0, tok * width), (tokens, width)) for e in layers]
    others = []
    for r in range(1, toks):
        to = (tok + r) % toks
        piece = jnp.stack(
            [lax.dynamic_slice(e, (member * rows, to * width), (rows, width)) for e in layers]
        )
        piece = tok_shift(piece, r)
        others.append(lax.all_gather(piece, "dst", axis_index_groups=members, axis=1, tiled=True))
    wide = [[own[j]] + [o[j] for o in others] for j in range(ahead)]

    size = features // CHUNKS
    codes, previous = [], []
    for c in range(CHUNKS):
        columns = slice(c * size, (c + 1) * size)
        scaled = latents[:, columns] * per_step[None, columns] + 0.5
        code = (jnp.minimum(scaled.astype(jnp.int32), 2 * HALF - 1) - HALF).astype(jnp.int16)
        codes.append(code.T)
        previous.append(group_shift(codes[-1], 1, 0, LAYERS - 2))
    step_previous = group_shift(step, 1, 0, LAYERS - 2)

    others_previous = [[tok_shift(p, r) for r in range(1, toks)] for p in previous]
    blocks, ends = [], []
    for c in range(CHUNKS):
        scale = step_previous[c * size:(c + 1) * size, None]
        theirs = [previous[c]] + others_previous[c]
        later = []
        for j in range(ahead - 1, 0, -1):
            sent = product(theirs, wide[j], scale)
            later.append(group_shift(sent, j, 1, LAYERS - 1 - j))
        ends.append(sent)
        blocks.append([product(theirs, wide[0], scale)] + later[::-1])

    bound = 6 * 0.125 * depth * (LAYERS - 1)
    raise_by = 1.0
    while raise_by * 2 * bound < 65504.0:
        raise_by = raise_by * 2
    span = features // SUM_CHUNKS
    sums = [None] * SUM_CHUNKS
    weights = []
    for c in range(SUM_CHUNKS):
        start = after(jnp.int32(c * span), codes[-1])
        part = lax.optimization_barrier(lax.dynamic_slice_in_dim(decoder, start, span, 0))
        weights.append([part[:, k, :] for k in range(LAYERS)])
    for distance in range(LAYERS - 1, -1, -1):
        valid = (distance <= my_group).astype(jnp.float32)
        for c in range(SUM_CHUNKS):
            lhs = layers[0]
            if sums[c] is not None:
                if distance == LAYERS - 2:
                    sums[c] = after(sums[c], ends[(c + 1) * CHUNKS // SUM_CHUNKS - 1])
                lhs = after(lhs, sums[c])
            term = valid * lax.dot_general(
                lhs, weights[c][distance], (((1,), (1,)), ((), ())),
                preferred_element_type=jnp.float32,
            )
            if sums[c] is not None:
                term = term + sums[c].astype(jnp.float32) * (1.0 / raise_by)
            if distance:
                sums[c] = group_shift(
                    (term * raise_by).astype(jnp.float16), -1, distance, LAYERS - 1
                )
            else:
                cut = mask[:, c * span:(c + 1) * span]
                sums[c] = cut.astype(jnp.float32) * term
    latent_grad = jnp.concatenate(sums, axis=1)

    decoder_grad = jnp.zeros((features, LAYERS, width), jnp.bfloat16)
    for c in range(CHUNKS):
        code = after(codes[c], previous[-1])
        mine = [after(codes[c], ends[-1])] + [tok_shift(code, r) for r in range(1, toks)]
        slots = [product(mine, wide[0], step[c * size:(c + 1) * size, None])] + blocks[c]
        block = with_layout_constraint(jnp.stack(slots, axis=1), Layout((0, 1, 2)))
        block = lax.optimization_barrier(block)
        decoder_grad = lax.dynamic_update_slice(decoder_grad, block, (c * size, 0, 0))
    return decoder_grad, latent_grad


def solution(mesh):
    placed = (P("tok", "dst"), P("tok", "dst"), P("tok", None, None), P("dst", None, None))
    return jax.shard_map(
        per_device,
        mesh=mesh,
        in_specs=placed,
        out_specs=(P("dst", None, "tok"), P("tok", "dst")),
        check_vma=False,
    )
```

time: 1600 us -> 787 us (0.49)
  waiting for transfers between devices: 1170 us -> 227 us
  local copies, waits for them, and re-layouts: 122 us -> 245 us
  matrix products: 198 us -> 85.9 us
  Pallas kernels: 0 us -> 95.9 us
  starting transfers between devices: 23.1 us -> 52.1 us
    ppermute x6 -> x35, waiting for transfers between devices: 966 us -> 227 us  [the longest x10 120 us: tok_shift(): lax.ppermute(array, 'tok', [(i, (i + by) % peers) for i in range(peers)])]
    reduce_scatter x1 -> x0, waiting for transfers between devices: 207 us -> none  [per_device(): totals = lax.psum_scatter(terms, 'tok', scatter_dimension=2, tiled=True)]
    dot_general x8 -> x16, matrix products: 198 us -> 85.9 us  [per_device(): lax.dot_general(lhs, weights[c][distance], (((1,), (1,)), ((), ())), pref...]
    pallas_call x0 -> x16, Pallas kernels: none -> 95.9 us  [product(): pl.pallas_call(lambda *refs: product_kernel(parts, *refs), grid=(features...]
    slice x1 -> x3, local copies, waits for them, and re-layouts: 79.6 us -> 2.98 us  [the longest x1 2.97 us: per_device(): scaled = latents[:, columns] * per_step[None, columns] + 0.5]
    dynamic_slice x1 -> x4, local copies, waits for them, and re-layouts: 10.4 us -> 74.6 us  [the longest x1 29.3 us: per_device(): lax.dynamic_slice_in_dim(decoder, start, span, 0)]
    another operation x0 -> x17, local copies, waits for them, and re-layouts: none -> 44.4 us  [the longest x16 44 us: per_device(): block = with_layout_constraint(jnp.stack(slots, axis=1), Layout((0, 1, 2)))]
    unnamed x6 -> x87, local copies, waits for them, and re-layouts: 31.8 us -> 74.1 us
  transfers between devices with their start and end apart: 7 -> 36, of which waited for: 7 -> 12; matrix products, arithmetic and copies ran while one was open for 16% -> 46% of each run, Pallas kernels for 0% -> 12%
where the time goes in v1:
time: 787 us; the launch traced here: 777 us
  local copies, waits for them, and re-layouts  245 us (31%)
  waiting for transfers between devices  227 us (29%)
  Pallas kernels  95.9 us (12%)
  matrix products  85.9 us (11%)
  other arithmetic  56.1 us (7%)
  starting transfers between devices  52.1 us (7%)
  between operations  15.3 us (2%)
    ppermute x10, waiting for transfers between devices, tok_shift(): lax.ppermute(array, 'tok', [(i, (i + by) % peers) for i in range(peers)])  120 us
    ppermute x25, waiting for transfers between devices, group_shift(): return lax.ppermute(array, 'dst', pairs)  107 us
    pallas_call x16, Pallas kernels, product(): pl.pallas_call(lambda *refs: product_kernel(parts, *refs), grid=(features...  95.9 us
    dot_general x16, matrix products, per_device(): lax.dot_general(lhs, weights[c][distance], (((1,), (1,)), ((), ())), pref...  85.9 us
    unnamed x87, local copies, waits for them, and re-layouts  74.1 us
    ppermute x25, starting transfers between devices, group_shift(): return lax.ppermute(array, 'dst', pairs)  44.5 us
    another operation x16, local copies, waits for them, and re-layouts, per_device(): block = with_layout_constraint(jnp.stack(slots, axis=1), Layout((0, 1, 2)))  44 us
    another operation x4, other arithmetic, per_device(): block = with_layout_constraint(jnp.stack(slots, axis=1), Layout((0, 1, 2)))  39.8 us
  transfers between devices with their start and end apart: 36, of which 12 were waited for; matrix products, arithmetic and copies ran while one was open for 46% of the time, Pallas kernels for 12%

profile of v1, /device:TPU:0, one launch (start us, length us, event | category | flops | bytes accessed | tf_op | source)
XLA Modules:
  0.0 777.1 jit_solution(8844569047750507122)
XLA Ops:
  18.9 34.5 %collective-permute-done.4 = bf16[3,256,1024]{2,1,0:T(8,128)(2,1)S(1)} collective-permute-done((bf16[3,256,1024]{2,1,0:T(8,128)(2,1)S(1)}, bf16[3,256,1024]{2,1,0:T(8,128)(2,1)S(1)}, u32[]{:S(2)}, u32[]{:S(2)}) %collective-permute-start.4) | collective-permute-done | bytes 1572896 | tf_op jit(solution)/shard_map/ppermute | solution.py:29
  60.2 11.7 %constant_dynamic-slice_fusion.4 = bf16[1024,1,2048]{2,1,0:T(2,128)(2,1)} fusion(bf16[1024,4,2048]{2,1,0:T(4,128)(2,1)} %param.6, s32[]{:T(128)S(6)} %select_n.72), kind=kLoop, calls=%fused_computation.79 | loop fusion | bytes 8388612 | tf_op jit(solution)/shard_map/jit(dynamic_index_in_dim)/dynamic_slice | solution.py:92
  71.9 25.8 %constant_dynamic-slice_fusion.6 = (bf16[1024,1,1024]{2,1,0:T(2,128)(2,1)}, bf16[1024,1,1024]{2,1,0:T(2,128)(2,1)}, bf16[1024,1,1024]{2,1,0:T(2,128)(2,1)}) fusion(bf16[1024,4,2048]{2,1,0:T(4,128)(2,1)} %param.6, s32[]{:T(128)S(6)} %select_n.73, s32[]{:T(128)S(6)} %select_n.68, s32[]{:T(128)S(6)} %select_n.78, s32[]{:T(128)S(6)} %select_n.66), kind=kLoop, calls=%fused_computation.84 | loop fusion | bytes 12582928 | tf_op jit(solution)/shard_map/dynamic_slice | solution.py:96
  119.7 8.0 %copy.91 = bf16[1024,1,2048]{2,0,1:T(8,128)(2,1)} copy(bf16[1024,1,2048]{2,1,0:T(2,128)(2,1)} %constant_dynamic-slice_fusion.4) | data formatting | bytes 8388608
  152.4 29.3 %constant_dynamic-slice_fusion.3 = (bf16[512,4,2048]{2,1,0:T(4,128)(2,1)}, bf16[512,4,2048]{2,1,0:T(4,128)(2,1)}, bf16[512,4,2048]{2,1,0:T(4,128)(2,1)}, bf16[512,4,2048]{2,1,0:T(4,128)(2,1)}) fusion(bf16[2048,4,2048]{2,1,0:T(4,128)(2,1)} %param.7, s32[]{:T(128)S(6)} %select_n.79, s32[]{:T(128)S(6)} %select_n.81, s32[]{:T(128)S(6)} %select_n.80, s32[]{:T(128)S(6)} %select_n.82), kind=kLoop, calls=%fused_computation.78 | loop fusion | bytes 67108880 | tf_op jit(solution)/shard_map/dynamic_slice | solution.py:138
  181.7 11.4 %copy.83 = bf16[512,4,2048]{2,0,1:T(8,128)(2,1)} copy(bf16[512,4,2048]{2,1,0:T(4,128)(2,1)} %get-tuple-element.61) | data formatting | bytes 16777216
  193.0 11.3 %copy.82 = bf16[512,4,2048]{2,0,1:T(8,128)(2,1)} copy(bf16[512,4,2048]{2,1,0:T(4,128)(2,1)} %get-tuple-element.59) | data formatting | bytes 16777216
  204.4 11.5 %copy.81 = bf16[512,4,2048]{2,0,1:T(8,128)(2,1)} copy(bf16[512,4,2048]{2,1,0:T(4,128)(2,1)} %get-tuple-element.60) | data formatting | bytes 16777216
  215.9 11.3 %copy.80 = bf16[512,4,2048]{2,0,1:T(8,128)(2,1)} copy(bf16[512,4,2048]{2,1,0:T(4,128)(2,1)} %get-tuple-element.58) | data formatting | bytes 16777216
  276.3 16.4 %collective-permute-done.7.refs_2_ = s16[512,1024]{1,0:T(8,128)(2,1)} collective-permute-done((s16[512,1024]{1,0:T(8,128)(2,1)}, s16[512,1024]{1,0:T(8,128)(2,1)}, u32[]{:S(2)}, u32[]{:S(2)}) %collective-permute-start.7) | collective-permute-done | bytes 1048608 | tf_op jit(solution)/shard_map/ppermute | solution.py:29
  302.0 13.2 %collective-permute-done.5.refs_2_ = s16[512,1024]{1,0:T(8,128)(2,1)} collective-permute-done((s16[512,1024]{1,0:T(8,128)(2,1)}, s16[512,1024]{1,0:T(8,128)(2,1)}, u32[]{:S(2)}, u32[]{:S(2)}) %collective-permute-start.5) | collective-permute-done | bytes 1048608 | tf_op jit(solution)/shard_map/ppermute | solution.py:29
  324.5 13.0 %collective-permute-done.12.refs_2_ = s16[512,1024]{1,0:T(8,128)(2,1)S(1)} collective-permute-done((s16[512,1024]{1,0:T(8,128)(2,1)}, s16[512,1024]{1,0:T(8,128)(2,1)S(1)}, u32[]{:S(2)}, u32[]{:S(2)}) %collective-permute-start.12) | collective-permute-done | bytes 1048608 | tf_op jit(solution)/shard_map/ppermute | solution.py:29
  346.3 13.7 %collective-permute-done.10.refs_2_ = s16[512,1024]{1,0:T(8,128)(2,1)S(1)} collective-permute-done((s16[512,1024]{1,0:T(8,128)(2,1)}, s16[512,1024]{1,0:T(8,128)(2,1)S(1)}, u32[]{:S(2)}, u32[]{:S(2)}) %collective-permute-start.10) | collective-permute-done | bytes 1048608 | tf_op jit(solution)/shard_map/ppermute | solution.py:29
  370.4 12.1 %collective-permute-done.17.refs_2_ = s16[512,1024]{1,0:T(8,128)(2,1)S(1)} collective-permute-done((s16[512,1024]{1,0:T(8,128)(2,1)}, s16[512,1024]{1,0:T(8,128)(2,1)S(1)}, u32[]{:S(2)}, u32[]{:S(2)}) %collective-permute-start.17) | collective-permute-done | bytes 1048608 | tf_op jit(solution)/shard_map/ppermute | solution.py:29
  393.0 9.2 %collective-permute-done.15.refs_2_ = s16[512,1024]{1,0:T(8,128)(2,1)S(1)} collective-permute-done((s16[512,1024]{1,0:T(8,128)(2,1)}, s16[512,1024]{1,0:T(8,128)(2,1)S(1)}, u32[]{:S(2)}, u32[]{:S(2)}) %collective-permute-start.15) | collective-permute-done | bytes 1048608 | tf_op jit(solution)/shard_map/ppermute | solution.py:29
  535.5 10.2 %pad_maximum_fusion.1 = bf16[512,4,1024]{2,1,0:T(4,128)(2,1)S(1)} fusion(bf16[512,1,1024]{2,1,0:T(2,128)(2,1)S(1)} %copy.30, bf16[512,1,1024]{2,1,0:T(2,128)(2,1)S(1)} %copy.29, bf16[512,1,1024]{2,1,0:T(2,128)(2,1)S(1)} %copy.28, bf16[512,1,1024]{2,1,0:T(2,128)(2,1)S(1)} %copy-done.15), kind=kLoop, calls=%fused_computation.1 | loop fusion | flops 16777216 | bytes 8388608 | tf_op jit(solution)/shard_map/stack | solution.py:168
  545.8 9.8 %pad_maximum_fusion.2 = bf16[512,4,1024]{2,1,0:T(4,128)(2,1)S(1)} fusion(bf16[512,1,1024]{2,1,0:T(2,128)(2,1)S(1)} %copy.39, bf16[512,1,1024]{2,1,0:T(2,128)(2,1)S(1)} %copy.38, bf16[512,1,1024]{2,1,0:T(2,128)(2,1)S(1)} %copy-done.16, bf16[512,1,1024]{2,1,0:T(2,128)(2,1)S(1)} %copy-done.17), kind=kLoop, calls=%fused_computation.2 | loop fusion | flops 16777216 | bytes 8388608 | tf_op jit(solution)/shard_map/stack | solution.py:168
  555.6 9.8 %pad_maximum_fusion.3 = bf16[512,4,1024]{2,1,0:T(4,128)(2,1)S(1)} fusion(bf16[512,1,1024]{2,1,0:T(2,128)(2,1)S(1)} %copy-done.21, bf16[512,1,1024]{2,1,0:T(2,128)(2,1)S(1)} %copy-done.22, bf16[512,1,1024]{2,1,0:T(2,128)(2,1)S(1)} %copy-done.18, bf16[512,1,1024]{2,1,0:T(2,128)(2,1)S(1)} %copy-done.20), kind=kLoop, calls=%fused_computation.3 | loop fusion | flops 16777216 | bytes 8388608 | tf_op jit(solution)/shard_map/stack | solution.py:168
  565.5 10.0 %pad_maximum_fusion.4 = bf16[512,4,1024]{2,1,0:T(4,128)(2,1)S(1)} fusion(bf16[512,1,1024]{2,1,0:T(2,128)(2,1)S(1)} %copy-done.23, bf16[512,1,1024]{2,1,0:T(2,128)(2,1)S(1)} %copy-done.24, bf16[512,1,1024]{2,1,0:T(2,128)(2,1)S(1)} %copy-done.19, bf16[512,1,1024]{2,1,0:T(2,128)(2,1)S(1)} %copy.52), kind=kLoop, calls=%fused_computation.4 | loop fusion | flops 16777216 | bytes 8388608 | tf_op jit(solution)/shard_map/stack | solution.py:168
  602.1 28.3 %dynamic_update_slice.12 = bf16[2048,4,1024]{2,1,0:T(4,128)(2,1)} pad(bf16[512,4,1024]{2,1,0:T(4,128)(2,1)S(1)} %pad_maximum_fusion.1, bf16[]{:T(256)} %constant.179.clone.1), padding=0_1536x0_0x0_0 | pad | bytes 20971522 | tf_op jit(solution)/shard_map/dynamic_update_slice | solution.py:170
  640.8 43.2 %collective-permute-done.34 = f16[1024,512]{1,0:T(8,128)(2,1)} collective-permute-done((f16[1024,512]{1,0:T(8,128)(2,1)}, f16[1024,512]{1,0:T(8,128)(2,1)}, u32[]{:S(2)}, u32[]{:S(2)}) %collective-permute-start.34) | collective-permute-done | bytes 1048608 | tf_op jit(solution)/shard_map/ppermute | solution.py:24
  684.0 22.4 %collective-permute-done.31 = f16[1024,512]{1,0:T(8,128)(2,1)S(1)} collective-permute-done((f16[1024,512]{1,0:T(8,128)(2,1)}, f16[1024,512]{1,0:T(8,128)(2,1)S(1)}, u32[]{:S(2)}, u32[]{:S(2)}) %collective-permute-start.31) | collective-permute-done | bytes 1048608 | tf_op jit(solution)/shard_map/ppermute | solution.py:24
  706.4 22.6 %collective-permute-done.28 = f16[1024,512]{1,0:T(8,128)(2,1)} collective-permute-done((f16[1024,512]{1,0:T(8,128)(2,1)}, f16[1024,512]{1,0:T(8,128)(2,1)}, u32[]{:S(2)}, u32[]{:S(2)}) %collective-permute-start.28) | collective-permute-done | bytes 1048608 | tf_op jit(solution)/shard_map/ppermute | solution.py:24
  729.0 19.3 %collective-permute-done.25 = f16[1024,512]{1,0:T(8,128)(2,1)} collective-permute-done((f16[1024,512]{1,0:T(8,128)(2,1)}, f16[1024,512]{1,0:T(8,128)(2,1)}, u32[]{:S(2)}, u32[]{:S(2)}) %collective-permute-start.25) | collective-permute-done | bytes 1048608 | tf_op jit(solution)/shard_map/ppermute | solution.py:24
  (220 shorter events, 353.9 us)
Async XLA Ops:
  7.2 250.0 %all-gather.2.cloned.1.call-start = ((), (), s32[]{:S(2)}) async-start(), calls=%async_computation | async-start | bytes 7864320 | tf_op jit(solution)/shard_map/all_gather | solution.py:104
  58.4 69.4 %collective-permute-start = (f32[2048]{0:T(1024)S(1)}, f32[2048]{0:T(1024)S(1)}, u32[]{:S(2)}, u32[]{:S(2)}) collective-permute-start(f32[2048]{0:T(1024)S(1)} %reduce_max.9), channel_id=1, source_target_pairs={{0,1},{1,0},{2,3},{3,2},{4,5},{5,4},{6,7},{7,6},{8,9},{9,8},{10,11... | collective-permute-start | bytes 24584 | tf_op jit(solution)/shard_map/ppermute | solution.py:29
  127.8 125.9 %collective-permute-start.1 = (f32[2048]{0:T(1024)S(1)}, f32[2048]{0:T(1024)S(1)}, u32[]{:S(2)}, u32[]{:S(2)}) collective-permute-start(f32[2048]{0:T(1024)S(1)} %get-tuple-element.76), channel_id=1, source_target_pairs={{0,8},{2,10},{4,12},{6,14},{8,16},{10,18},{12,20},{14,22},{16,24},... | collective-permute-start | bytes 24584 | tf_op jit(solution)/shard_map/ppermute | solution.py:24
  133.2 110.6 %collective-permute-start.2 = (s16[512,1024]{1,0:T(8,128)(2,1)S(1)}, s16[512,1024]{1,0:T(8,128)(2,1)}, u32[]{:S(2)}, u32[]{:S(2)}) collective-permute-start(s16[512,1024]{1,0:T(8,128)(2,1)S(1)} %fusion.17.refs_1_), channel_id=1, source_target_pairs={{0,8},{2,10},{4,12},{6,14},{8,16},{10,18},{12,20},{14,22},{16,24},... | collective-permute-start | bytes 3145736 | tf_op jit(solution)/shard_map/ppermute | solution.py:24
  141.0 110.6 %collective-permute-start.6 = (s16[512,1024]{1,0:T(8,128)(2,1)}, s16[512,1024]{1,0:T(8,128)(2,1)}, u32[]{:S(2)}, u32[]{:S(2)}) collective-permute-start(s16[512,1024]{1,0:T(8,128)(2,1)} %fusion.16.refs_1_), channel_id=1, source_target_pairs={{0,8},{2,10},{4,12},{6,14},{8,16},{10,18},{12,20},{14,22},{16,24},... | collective-permute-start | bytes 3145736 | tf_op jit(solution)/shard_map/ppermute | solution.py:24
  146.3 114.6 %collective-permute-start.11 = (s16[512,1024]{1,0:T(8,128)(2,1)}, s16[512,1024]{1,0:T(8,128)(2,1)}, u32[]{:S(2)}, u32[]{:S(2)}) collective-permute-start(s16[512,1024]{1,0:T(8,128)(2,1)} %fusion.18.refs_1_), channel_id=1, source_target_pairs={{0,8},{2,10},{4,12},{6,14},{8,16},{10,18},{12,20},{14,22},{16,24},... | collective-permute-start | bytes 3145736 | tf_op jit(solution)/shard_map/ppermute | solution.py:24
  150.1 150.2 %collective-permute-start.16 = (s16[512,1024]{1,0:T(8,128)(2,1)}, s16[512,1024]{1,0:T(8,128)(2,1)}, u32[]{:S(2)}, u32[]{:S(2)}) collective-permute-start(s16[512,1024]{1,0:T(8,128)(2,1)} %fusion.19.refs_1_), channel_id=1, source_target_pairs={{0,8},{2,10},{4,12},{6,14},{8,16},{10,18},{12,20},{14,22},{16,24},... | collective-permute-start | bytes 3145736 | tf_op jit(solution)/shard_map/ppermute | solution.py:24
  260.9 165.8 %collective-permute-start.32 = (f16[1024,512]{1,0:T(8,128)(2,1)S(1)}, f16[1024,512]{1,0:T(8,128)(2,1)}, u32[]{:S(2)}, u32[]{:S(2)}) collective-permute-start(f16[1024,512]{1,0:T(8,128)(2,1)S(1)} %copy-done.29), channel_id=1, source_target_pairs={{24,16},{26,18},{28,20},{30,22},{25,17},{27,19},{29,21},{31,23}} | collective-permute-start | bytes 3145736 | tf_op jit(solution)/shard_map/ppermute | solution.py:24
  270.2 67.3 %collective-permute-start.12 = (s16[512,1024]{1,0:T(8,128)(2,1)}, s16[512,1024]{1,0:T(8,128)(2,1)S(1)}, u32[]{:S(2)}, u32[]{:S(2)}) collective-permute-start(s16[512,1024]{1,0:T(8,128)(2,1)} %collective-permute-done.11.refs_1_), channel_id=1, source_target_pairs={{0,1},{1,0},{2,3},{3,2},{4,5},{5,4},{6,7},{7,6},{8,9},{9,8},{10,11... | collective-permute-start | bytes 3145736 | tf_op jit(solution)/shard_map/ppermute | solution.py:29
  292.7 67.3 %collective-permute-start.10 = (s16[512,1024]{1,0:T(8,128)(2,1)}, s16[512,1024]{1,0:T(8,128)(2,1)S(1)}, u32[]{:S(2)}, u32[]{:S(2)}) collective-permute-start(s16[512,1024]{1,0:T(8,128)(2,1)} %fusion.18.refs_1_), channel_id=1, source_target_pairs={{0,1},{1,0},{2,3},{3,2},{4,5},{5,4},{6,7},{7,6},{8,9},{9,8},{10,11... | collective-permute-start | bytes 3145736 | tf_op jit(solution)/shard_map/ppermute | solution.py:29
  300.3 140.6 %collective-permute-start.29 = (f16[1024,512]{1,0:T(8,128)(2,1)}, f16[1024,512]{1,0:T(8,128)(2,1)}, u32[]{:S(2)}, u32[]{:S(2)}) collective-permute-start(f16[1024,512]{1,0:T(8,128)(2,1)} %multiply_convert_fusion.5), channel_id=1, source_target_pairs={{24,16},{26,18},{28,20},{30,22},{25,17},{27,19},{29,21},{31,23}} | collective-permute-start | bytes 3145736 | tf_op jit(solution)/shard_map/ppermute | solution.py:24
  315.2 67.3 %collective-permute-start.17 = (s16[512,1024]{1,0:T(8,128)(2,1)}, s16[512,1024]{1,0:T(8,128)(2,1)S(1)}, u32[]{:S(2)}, u32[]{:S(2)}) collective-permute-start(s16[512,1024]{1,0:T(8,128)(2,1)} %collective-permute-done.16.refs_1_), channel_id=1, source_target_pairs={{0,1},{1,0},{2,3},{3,2},{4,5},{5,4},{6,7},{7,6},{8,9},{9,8},{10,11... | collective-permute-start | bytes 3145736 | tf_op jit(solution)/shard_map/ppermute | solution.py:29
  337.5 64.6 %collective-permute-start.15 = (s16[512,1024]{1,0:T(8,128)(2,1)}, s16[512,1024]{1,0:T(8,128)(2,1)S(1)}, u32[]{:S(2)}, u32[]{:S(2)}) collective-permute-start(s16[512,1024]{1,0:T(8,128)(2,1)} %fusion.19.refs_1_), channel_id=1, source_target_pairs={{0,1},{1,0},{2,3},{3,2},{4,5},{5,4},{6,7},{7,6},{8,9},{9,8},{10,11... | collective-permute-start | bytes 3145736 | tf_op jit(solution)/shard_map/ppermute | solution.py:29
  360.0 107.7 %collective-permute-start.26 = (f16[1024,512]{1,0:T(8,128)(2,1)}, f16[1024,512]{1,0:T(8,128)(2,1)}, u32[]{:S(2)}, u32[]{:S(2)}) collective-permute-start(f16[1024,512]{1,0:T(8,128)(2,1)} %multiply_convert_fusion.8), channel_id=1, source_target_pairs={{24,16},{26,18},{28,20},{30,22},{25,17},{27,19},{29,21},{31,23}} | collective-permute-start | bytes 3145736 | tf_op jit(solution)/shard_map/ppermute | solution.py:24
  382.5 104.2 %collective-permute-start.23 = (f16[1024,512]{1,0:T(8,128)(2,1)}, f16[1024,512]{1,0:T(8,128)(2,1)}, u32[]{:S(2)}, u32[]{:S(2)}) collective-permute-start(f16[1024,512]{1,0:T(8,128)(2,1)} %multiply_convert_fusion.11), channel_id=1, source_target_pairs={{24,16},{26,18},{28,20},{30,22},{25,17},{27,19},{29,21},{31,23}} | collective-permute-start | bytes 3145736 | tf_op jit(solution)/shard_map/ppermute | solution.py:24
  402.2 85.4 %collective-permute-start.20 = (s16[512,1024]{1,0:T(8,128)(2,1)S(1)}, s16[512,1024]{1,0:T(8,128)(2,1)}, u32[]{:S(2)}, u32[]{:S(2)}) collective-permute-start(s16[512,1024]{1,0:T(8,128)(2,1)S(1)} %fusion.17.refs_1_), channel_id=1, source_target_pairs={{0,1},{1,0},{2,3},{3,2},{4,5},{5,4},{6,7},{7,6},{8,9},{9,8},{10,11... | collective-permute-start | bytes 3145736 | tf_op jit(solution)/shard_map/ppermute | solution.py:29
  512.6 62.8 %collective-permute-start.33 = (f16[1024,512]{1,0:T(8,128)(2,1)}, f16[1024,512]{1,0:T(8,128)(2,1)}, u32[]{:S(2)}, u32[]{:S(2)}) collective-permute-start(f16[1024,512]{1,0:T(8,128)(2,1)} %multiply_convert_fusion.1), channel_id=1, source_target_pairs={{16,8},{18,10},{20,12},{22,14},{24,16},{26,18},{28,20},{30,22},{17... | collective-permute-start | bytes 3145736 | tf_op jit(solution)/shard_map/ppermute | solution.py:24
  516.3 65.9 %collective-permute-start.30 = (f16[1024,512]{1,0:T(8,128)(2,1)S(1)}, f16[1024,512]{1,0:T(8,128)(2,1)}, u32[]{:S(2)}, u32[]{:S(2)}) collective-permute-start(f16[1024,512]{1,0:T(8,128)(2,1)S(1)} %copy-done.30), channel_id=1, source_target_pairs={{16,8},{18,10},{20,12},{22,14},{24,16},{26,18},{28,20},{30,22},{17... | collective-permute-start | bytes 3145736 | tf_op jit(solution)/shard_map/ppermute | solution.py:24
  522.1 66.7 %collective-permute-start.27 = (f16[1024,512]{1,0:T(8,128)(2,1)}, f16[1024,512]{1,0:T(8,128)(2,1)}, u32[]{:S(2)}, u32[]{:S(2)}) collective-permute-start(f16[1024,512]{1,0:T(8,128)(2,1)} %multiply_convert_fusion.7), channel_id=1, source_target_pairs={{16,8},{18,10},{20,12},{22,14},{24,16},{26,18},{28,20},{30,22},{17... | collective-permute-start | bytes 3145736 | tf_op jit(solution)/shard_map/ppermute | solution.py:24
  526.7 68.7 %collective-permute-start.24 = (f16[1024,512]{1,0:T(8,128)(2,1)}, f16[1024,512]{1,0:T(8,128)(2,1)}, u32[]{:S(2)}, u32[]{:S(2)}) collective-permute-start(f16[1024,512]{1,0:T(8,128)(2,1)} %multiply_convert_fusion.10), channel_id=1, source_target_pairs={{16,8},{18,10},{20,12},{22,14},{24,16},{26,18},{28,20},{30,22},{17... | collective-permute-start | bytes 3145736 | tf_op jit(solution)/shard_map/ppermute | solution.py:24
  580.8 103.2 %collective-permute-start.34 = (f16[1024,512]{1,0:T(8,128)(2,1)}, f16[1024,512]{1,0:T(8,128)(2,1)}, u32[]{:S(2)}, u32[]{:S(2)}) collective-permute-start(f16[1024,512]{1,0:T(8,128)(2,1)} %multiply_convert_fusion), channel_id=1, source_target_pairs={{8,0},{10,2},{12,4},{14,6},{16,8},{18,10},{20,12},{22,14},{24,16},... | collective-permute-start | bytes 3145736 | tf_op jit(solution)/shard_map/ppermute | solution.py:24
  587.5 118.9 %collective-permute-start.31 = (f16[1024,512]{1,0:T(8,128)(2,1)}, f16[1024,512]{1,0:T(8,128)(2,1)S(1)}, u32[]{:S(2)}, u32[]{:S(2)}) collective-permute-start(f16[1024,512]{1,0:T(8,128)(2,1)} %multiply_convert_fusion.3), channel_id=1, source_target_pairs={{8,0},{10,2},{12,4},{14,6},{16,8},{18,10},{20,12},{22,14},{24,16},... | collective-permute-start | bytes 3145736 | tf_op jit(solution)/shard_map/ppermute | solution.py:24
  594.1 134.8 %collective-permute-start.28 = (f16[1024,512]{1,0:T(8,128)(2,1)}, f16[1024,512]{1,0:T(8,128)(2,1)}, u32[]{:S(2)}, u32[]{:S(2)}) collective-permute-start(f16[1024,512]{1,0:T(8,128)(2,1)} %multiply_convert_fusion.6), channel_id=1, source_target_pairs={{8,0},{10,2},{12,4},{14,6},{16,8},{18,10},{20,12},{22,14},{24,16},... | collective-permute-start | bytes 3145736 | tf_op jit(solution)/shard_map/ppermute | solution.py:24
  600.8 147.4 %collective-permute-start.25 = (f16[1024,512]{1,0:T(8,128)(2,1)}, f16[1024,512]{1,0:T(8,128)(2,1)}, u32[]{:S(2)}, u32[]{:S(2)}) collective-permute-start(f16[1024,512]{1,0:T(8,128)(2,1)} %multiply_convert_fusion.9), channel_id=1, source_target_pairs={{8,0},{10,2},{12,4},{14,6},{16,8},{18,10},{20,12},{22,14},{24,16},... | collective-permute-start | bytes 3145736 | tf_op jit(solution)/shard_map/ppermute | solution.py:24
  (49 other events, 1060.0 us)
Sparse Core Ops, SparseCore 0:
  54.7 47.9 all-gather.1
